TPU v7x, 32 devices: a whole 2x2x4 slice. The times are simulated.
32 devices in a mesh: dp: 16 (over z, y, x), mp: 2 (over core).
Axes of the slice: x: 2, y: 2, z: 4, core: 2. Of those that a mesh axis runs over, the one named last changes fastest.
Arguments:
- tokens: bfloat16 [65536, 512], P(('dp', 'mp')), may hold values from -6 to 6
- segment_ids: int32 [128, 512], P('dp'), may hold values from 0 to 7, never falling along the last dimension, each value on 1 to 256 neighbouring positions
- cotangent: bfloat16 [65536, 512], P(('dp', 'mp')), may hold values from -6 to 6
- pos_table: bfloat16 [512, 512], replicated, may hold values from -3 to 3
- w_qkv: bfloat16 [512, 1536], P(None, 'mp'), may hold values from -0.25 to 0.25
- w_out: bfloat16 [512, 512], P('mp'), may hold values from -1 to 1
- w_up: bfloat16 [512, 2048], P(None, 'mp'), may hold values from -0.25 to 0.25
- w_down: bfloat16 [2048, 512], P('mp'), may hold values from -0.125 to 0.125
- gain_one: float32 [512], replicated, may hold values from 0.5 to 1.5
- bias_one: float32 [512], replicated, may hold values from -1 to 1
- gain_two: float32 [512], replicated, may hold values from 0.5 to 1.5
- bias_two: float32 [512], replicated, may hold values from -1 to 1
Outputs:
- output: bfloat16 [65536, 512], P(('dp', 'mp'))
- input_grad: bfloat16 [65536, 512], P(('dp', 'mp'))
- pos_grad: float32 [512, 512], replicated
- qkv_grad: float32 [512, 1536], P(None, 'mp')
- out_grad: float32 [512, 512], P('mp')
- up_grad: float32 [512, 2048], P(None, 'mp')
- down_grad: float32 [2048, 512], P('mp')
- gain_one_grad: float32 [512], replicated
- bias_one_grad: float32 [512], replicated
- gain_two_grad: float32 [512], replicated
- bias_two_grad: float32 [512], replicated
Inputs may be any that keep to these rules, and one draw needn't show every extreme that they name: `segment_ids`: within each window the numbers never fall, and each number covers 1 to 256 consecutive characters.
All inputs are finite; a program needn't handle non-finite values.
Results may differ from a plain program's by a relative error of at most 0.017.
Values may be sent and summed in bfloat16 or wider, within the bound.
A program may use at most 192 MiB of HBM per device.

v0:
```python
import functools

import jax
import jax.numpy as jnp
from jax import lax
from jax.experimental import pallas as pl
from jax.experimental.pallas import tpu as pltpu
from jax.sharding import PartitionSpec as P

BF = jnp.bfloat16
F32 = jnp.float32
MESH = pl.DeviceIdType.MESH
HD = 64
EPSILON = 1e-05
NEG = -1e30
GELU_A = 0.7978845608028654
GELU_B = 0.044715

CHUNKS = {
    "D0": (32, 512),
    "D1": (32, 512),
    "U0": (32, 512),
    "U1": (32, 512),
    "O": (16, 512),
    "Q0": (32, 384),
    "QA": (16, 384),
    "QB": (16, 384),
    "P": (16, 512),
}
NAMES = tuple(CHUNKS)
DIRECT = ("QA", "QB", "P")
RESULTS = ("D0", "D1", "U0", "U1", "O", "Q0", "Q1", "P")
PIECES = 16

SCHEDULE = {
    ("down", 1): (("D0", 0),),
    ("down", 3): (("D1", 0),),
    ("slope", 0): (("D0", 1),),
    ("slope", 1): (("D1", 1),),
    ("up", 1): (("D0", 2), ("U0", 0),),
    ("up", 3): (("D1", 2), ("U0", 1), ("U1", 0),),
    ("nb", 0): (("D0", 3),),
    ("nb", 1): (("U1", 1),),
    ("nb", 2): (("D1", 3),),
    ("nb", 3): (("D0", 4), ("U0", 2),),
    ("O", 0): (("O", 0), ("sm", 0),),
    ("back0", 1): (("D1", 4), ("U1", 2), ("O", 1), ("sm", 1),),
    ("back0", 2): (("U0", 3),),
    ("back0", 3): (("D0", 5),),
    ("back1", 0): (("sm", 2),),
    ("back1", 1): (("D1", 5), ("U1", 3),),
    ("back1", 2): (("O", 2),),
    ("back1", 3): (("D0", 6), ("U0", 4), ("sm", 3),),
    ("q1", 0): (("D1", 6), ("U1", 4), ("Q0", 0),),
    ("add1", 0): (("O", 3),),
    ("back2", 0): (("sm", 4),),
    ("back2", 1): (("U0", 5), ("Q0", 1),),
    ("back2", 2): (("D0", 7),),
    ("back2", 3): (("U1", 5),),
    ("q2", 0): (("D1", 7), ("O", 4), ("QA", 0),),
    ("add2", 0): (("U0", 6),),
    ("back3", 1): (("Q0", 2), ("QA", 1),),
    ("back3", 2): (("U1", 6), ("O", 5),),
    ("P", 0): (("P", 0),),
    ("q3", 0): (("U0", 7), ("Q0", 3), ("QB", 0),),
    ("fin", 0): (("QA", 2), ("P", 1),),
    ("fin", 1): (("QB", 1),),
    ("fin", 3): (("U1", 7), ("Q0", 4),),
}
TAIL = (
    ("O", 6),
    ("QA", 3),
    ("P", 2),
    ("Q0", 5),
    ("QB", 2),
    ("QA", 4),
    ("O", 7),
    ("P", 3),
    ("QB", 3),
    ("Q0", 6),
    ("P", 4),
    ("QA", 5),
    ("QB", 4),
    ("QA", 6),
    ("Q0", 7),
    ("P", 5),
    ("P", 6),
    ("QB", 5),
    ("QB", 6),
)


def dot(left, right, left_dim=1, right_dim=0):
    return lax.dot_general(
        left, right, (((left_dim,), (right_dim,)), ((), ())), preferred_element_type=F32
    )


def lanes(shape):
    return lax.broadcasted_iota(jnp.int32, shape, len(shape) - 1)


def rows_of(w, win):
    return pl.ds(pl.multiple_of(w * win, win), win)


def columns_of(start, size):
    return pl.ds(pl.multiple_of(start, 128), size)


def row_mean(v):
    return jnp.mean(v, axis=-1, keepdims=True)


def kernel(fused, dims, *refs):
    win, width, hidden, windows = dims
    half_hidden = hidden // 2
    half = win // 2
    (tok_h, cot_h, pos_h, seg, wq_h, wo_h, wu_h, wd_h, g1, b1, g2, b2) = refs[:12]
    refs = refs[12:]
    out_h, ig_h, small_h = refs[:3]
    results = RESULTS if fused else NAMES
    F = dict(zip(results, refs[3 : 3 + len(results)]))
    b = dict(zip(scratch_of(fused, dims), refs[3 + len(results) :]))
    tok, cot, pos, augk = b["tok"], b["cot"], b["pos"], b["augk"]
    wq, wo, wu, wd = b["wq"], b["wo"], b["wu"], b["wd"]
    joined, mix, u1, rs1, pb, nb = b["joined"], b["mix"], b["u1"], b["rs1"], b["pb"], b["nb"]
    act, gp, augq, nf, small = b["act"], b["gp"], b["augq"], b["nf"], b["small"]
    G, R_mp, R_a, R_b, R_z = ({k: b.get(buf + k) for k in NAMES} for buf in ("G", "M", "A", "B", "Z"))
    in_sem, out_sem = b["in_sem"], b["out_sem"]

    pairs = width // 128

    copies = {}

    def fetch(name, src, dst, k):
        copies[name] = pltpu.make_async_copy(src, dst, in_sem.at[k])
        copies[name].start()

    if fused:
        wsem, csend, crecv, ssend, srecv, lsem = (
            b[k] for k in ("wsem", "csend", "crecv", "ssend", "srecv", "lsem")
        )
        dp = lax.axis_index("dp")
        mp = lax.axis_index("mp")
        zc = dp // 4
        yc = lax.rem(dp // 2, 2)
        xc = lax.rem(dp, 2)
        ac = jnp.where(mp == 0, xc, yc)
        bc = jnp.where(mp == 0, yc, xc)
        step_a = jnp.where(mp == 0, 1, 2)
        step_b = jnp.where(mp == 0, 2, 1)
        dev_mp = (dp, 1 - mp)
        dev_a = (dp + step_a * (1 - 2 * ac), mp)
        dev_b = (dp + step_b * (1 - 2 * bc), mp)
        dev_d = (dp + step_a * (1 - 2 * ac) + step_b * (1 - 2 * bc), mp)
        dev_x = (dp + 1 - 2 * xc, mp)
        dev_y = (dp + 2 * (1 - 2 * yc), mp)
        zs = [lax.rem(zc + k, 4) for k in (1, 2, 3)]
        dev_z = [(lax.rem(dp, 4) + 4 * z, mp) for z in zs]
        barrier = pltpu.get_barrier_semaphore()
        for dev in [dev_mp, dev_a, dev_b, dev_d] + dev_z:
            pl.semaphore_signal(barrier, inc=1, device_id=dev, device_id_type=MESH)

    raw_width = wq_h.shape[1]
    raw = act.at[pl.ds(0, width), pl.ds(0, raw_width)]
    fetch("wq", wq_h, raw, 2)
    fetch("tok", tok_h, tok, 0)
    fetch("pos", pos_h, pos, 1)
    wparts = []
    if fused:
        wparts.append((wo_h, wo.at[pl.ds(pl.multiple_of(mp * half, half), half), :]))
        wparts.append((wu_h, wu.at[:, columns_of(half_hidden * mp, half_hidden)]))
        wparts.append((wd_h, wd.at[pl.ds(pl.multiple_of(mp * half_hidden, half_hidden), half_hidden), :]))
    else:
        wparts += [(wo_h, wo), (wu_h, wu), (wd_h, wd)]
    for i, (src, dst) in enumerate(wparts):
        fetch("w%d" % i, src, dst, 5 + i)
    fetch("cot", cot_h, cot, 4)
    small[...] = jnp.zeros_like(small)
    rs1[...] = jnp.zeros_like(rs1)

    l64 = lax.rem(lanes((win, 128)), HD)
    lo = lanes((win, 128)) < HD

    columns = seg[...].astype(F32).T
    mine = (mp if fused else 0) * windows
    for w in range(windows):
        R = pl.ds(w * win, win)
        column = jnp.sum(
            jnp.where(lanes(columns.shape) == mine + w, columns, 0.0), axis=1, keepdims=True
        ).astype(jnp.int32)
        augk[R, :] = jnp.where((l64 == column) | ((l64 >= 8) & (l64 < 11)), 1.0, 0.0).astype(BF)

    copies["wq"].wait()
    own_columns = mp * raw_width // 3 if fused else 0
    for p in range(raw_width // 384):
        cut = [raw[:, pl.ds(p * 384 + 128 * i, 128)] for i in range(3)]
        low = lanes((width, 128)) < HD
        swapped = [pltpu.roll(c.astype(F32), HD, 1).astype(BF) for c in cut]
        q = jnp.where(low, cut[0], cut[1]) * BF(HD**-0.5)
        k = jnp.where(low, swapped[0], swapped[2])
        v = jnp.where(low, cut[1], cut[2])
        for i, part in enumerate((q, k, v)):
            wq[:, columns_of(own_columns + width * i + 128 * p, 128)] = part

    wremote = []
    if fused:
        pl.semaphore_wait(barrier, 7)
        slices = [wq.at[:, columns_of(own_columns + width * i, raw_width // 3)] for i in range(3)]
        for i, (src, dst) in enumerate([(x, x) for x in slices] + wparts):
            c = pltpu.make_async_remote_copy(
                src_ref=src, dst_ref=dst, send_sem=wsem.at[0, i], recv_sem=wsem.at[1, i],
                device_id=dev_mp, device_id_type=MESH,
            )
            c.start()
            wremote.append(c)

    def remote(src, dst, send, recv, dev):
        return pltpu.make_async_remote_copy(
            src_ref=src, dst_ref=dst, send_sem=send, recv_sem=recv, device_id=dev, device_id_type=MESH
        )

    def add(mine, got):
        mine[...] = mine[...] + got[...]

    def exchange(name, k):
        if not fused:
            return
        c = NAMES.index(name)
        g = G[name]
        direct = name in DIRECT
        own = g.at[mp]
        base = ac * 8 + bc * 4
        full = g.at[1 - mp]

        def send(src, dst, i, dev):
            return remote(src, dst, csend.at[c, i], crecv.at[c, i], dev)

        def to_z(src, dst_of):
            return [send(src(j), dst_of(j), 3 + j, dev_z[j]) for j in range(3)]

        if direct:
            slots = R_a[name]
            places = [(1 - ac) * 8 + bc * 4, ac * 8 + (1 - bc) * 4, (1 - ac) * 8 + (1 - bc) * 4]
            plane = [dev_a, dev_b, dev_d]
            stages = [
                lambda: [send(full, R_mp[name], 0, dev_mp)],
                lambda: [send(own.at[pl.ds(places[j], 4)], slots.at[j], 6 + j, plane[j]) for j in range(3)],
                lambda: [send(own.at[base + zs[j]], R_z[name].at[j], 3 + j, dev_z[j]) for j in range(3)],
                lambda: [send(full.at[base + zc], full.at[base + zc], 9 + j, dev_z[j]) for j in range(3)],
                lambda: [send(full.at[pl.ds(base, 4)], full.at[pl.ds(base, 4)], 12 + j, plane[j]) for j in range(3)],
                lambda: [send(full, b["X" + name], 1, dev_mp)],
            ]
        else:
            stages = [
                lambda: [send(full, R_mp[name], 0, dev_mp)],
                lambda: [send(own.at[pl.ds((1 - ac) * 8, 8)], R_a[name], 1, dev_a)],
                lambda: [send(own.at[pl.ds(ac * 8 + (1 - bc) * 4, 4)], R_b[name], 2, dev_b)],
                lambda: [send(own.at[base + zs[j]], R_z[name].at[j], 3 + j, dev_z[j]) for j in range(3)],
                lambda: [send(full.at[base + zc], full.at[base + zc], 6 + j, dev_z[j]) for j in range(3)],
                lambda: [send(full.at[pl.ds(base, 4)], full.at[pl.ds(base, 4)], 9, dev_b)],
                lambda: [send(full.at[pl.ds(ac * 8, 8)], full.at[pl.ds(ac * 8, 8)], 10, dev_a)],
            ]
        if 0 < k <= len(stages):
            for copy in stages[k - 1]():
                copy.wait()
        if k == 1:
            add(own, R_mp[name])
        if direct and k == 2:
            at = own.at[pl.ds(base, 4)]
            at[...] = (
                (at[...].astype(F32) + slots[0].astype(F32)) + (slots[1].astype(F32) + slots[2].astype(F32))
            ).astype(BF)
        if not direct and k == 2:
            add(own.at[pl.ds(ac * 8, 8)], R_a[name])
        if not direct and k == 3:
            add(own.at[pl.ds(base, 4)], R_b[name])
        if k == (3 if direct else 4):
            total = own[base + zc].astype(F32)
            for j in range(3):
                total = total + R_z[name][j].astype(F32)
            if name[0] == "Q":
                q, kk, v = total[:, :128] * (HD**-0.5), total[:, 128:256], total[:, 256:]
                total = jnp.concatenate(
                    [q[:, :HD], kk[:, :HD], v[:, :HD], q[:, HD:], kk[:, HD:], v[:, HD:]], axis=1
                )
            full[base + zc] = total.astype(BF)
        if k < len(stages):
            for copy in stages[k]():
                copy.start()
        if k == len(stages):
            results_out(name, True)

    def results_out(name, start):
        full, i = G[name].at[1 - mp], 2 * NAMES.index(name)
        if name not in DIRECT:
            moves = [pltpu.make_async_copy(full, F[name], lsem.at[i])]
        else:
            to = F["P" if name == "P" else "Q1"]
            moves = [pltpu.make_async_copy(full, to.at[mp], lsem.at[i])]
            moves.append(pltpu.make_async_copy(b["X" + name], to.at[1 - mp], lsem.at[i + 1]))

        def go():
            for m in moves:
                m.start() if start else m.wait()

        if name[0] == "Q" and name != "Q0":
            pl.when(mp == ("QA", "QB").index(name))(go)
        else:
            go()

    def exchange_small(k):
        if not fused:
            return
        legs = [(b["s_mp"], dev_mp, 0), (b["s_x"], dev_x, 1), (b["s_y"], dev_y, 2)]
        if k > 0 and k <= 3:
            buf, dev, s = legs[k - 1]
            remote(small, buf, ssend.at[s], srecv.at[s], dev).wait()
            small[...] = small[...] + buf[...]
        if k < 3:
            buf, dev, s = legs[k]
            remote(small, buf, ssend.at[s], srecv.at[s], dev).start()
        zcs = [remote(small, b["s_z"].at[zc], ssend.at[3 + j], srecv.at[3 + j], dev_z[j]) for j in range(3)]
        if k == 3:
            b["s_z"][zc] = small[...]
            for z in zcs:
                z.start()
        if k == 4:
            for z in zcs:
                z.wait()
            small[...] = (b["s_z"][0] + b["s_z"][1]) + (b["s_z"][2] + b["s_z"][3])

    causal = jnp.where(lanes((half, half)) <= lax.broadcasted_iota(jnp.int32, (half, half), 0), 0.0, NEG)
    def attend(w, p):
        R = rows_of(w, win)
        Q, K, V = (joined[R, columns_of(width * i + p * 128, 128)] for i in range(3))
        ak = augk[R, :]
        ones = jnp.ones((win, 128), BF)
        zero = jnp.zeros((win, 128), BF)
        aq = jnp.where(l64 < 8, (ones - ak) * BF(NEG), zero)
        qs, ks, vs = [], [], []
        for h in range(2):
            mine = lo if h == 0 else ~lo
            qs.append(jnp.where(mine, Q, aq))
            ks.append(jnp.where(mine, K, ak))
            vs.append(jnp.concatenate([jnp.where(mine, V, zero), jnp.where(mine, ones, zero)], axis=1))
        for qb in range(2):
            kl = half * (qb + 1)
            es, ms = [], []
            for h in range(2):
                s = dot(qs[h][qb * half : (qb + 1) * half], ks[h][:kl], 1, 1)
                if qb == 0:
                    s = s + causal
                else:
                    s = jnp.concatenate([s[:, :half], s[:, half:] + causal], axis=1)
                m = jnp.max(s, axis=1, keepdims=True)
                es.append(jnp.exp(s - m).astype(BF))
                ms.append(m)
            ov = dot(jnp.concatenate(es, axis=1), jnp.concatenate([v[:kl] for v in vs], axis=0))
            total = ov[:, 128:]
            rr = pl.ds(pl.multiple_of(w * win + qb * half, half), half)
            mix[rr, columns_of(p * 128, 128)] = (ov[:, :128] / total).astype(BF)
            low = lo[:half]
            lse = jnp.where(low, ms[0], ms[1]) + jnp.log(total)
            x = -pltpu.roll(lse, HD, 1)
            hi = x.astype(BF)
            x = x - hi.astype(F32)
            mid = x.astype(BF)
            last = (x - mid.astype(F32)).astype(BF)
            l6 = l64[:half]
            a = aq[qb * half : (qb + 1) * half]
            a = jnp.where(l6 == 8, hi, a)
            a = jnp.where(l6 == 9, mid, a)
            augq[rr, columns_of(p * 128, 128)] = jnp.where(l6 == 10, last, a)

    copies["tok"].wait()
    copies["pos"].wait()

    def place(w, _):
        R = rows_of(w, win)
        pb[R, :] = (tok[R, :].astype(F32) + pos[...].astype(F32)).astype(BF)
        return 0

    lax.fori_loop(0, windows, place, 0)
    for part in range(2 if fused else 1):
        if part:
            for c in wremote[:3]:
                c.wait()
        span = width // 2 if fused else width
        start = (mp if part == 0 else 1 - mp) * span if fused else 0

        def project(w, _):
            R = rows_of(w, win)
            for i in range(3):
                cs = columns_of(width * i + start, span)
                joined[R, cs] = dot(pb[R, :], wq[:, cs]).astype(BF)
            return 0

        lax.fori_loop(0, windows, project, 0)

    def attend_window(w, _):
        for p in range(pairs):
            attend(w, p)
        return 0

    lax.fori_loop(0, windows, attend_window, 0)

    for i in range(3):
        copies["w%d" % i].wait()
    for c in wremote[3:]:
        c.wait()
    copies["cot"].wait()

    def feed(w, _):
        R = rows_of(w, win)
        r1 = (tok[R, :].astype(F32) + pos[...].astype(F32)) + dot(mix[R, :], wo[...])
        center = r1 - row_mean(r1)
        rstd = lax.rsqrt(row_mean(center * center) + EPSILON)
        unit = center * rstd
        u1[R, :] = unit.astype(BF)
        rs1[...] = jnp.where(lanes((win, 128)) == w, rstd, rs1[...])
        normed = unit * g1[...] + b1[...]
        nf[...] = normed
        nb[R, :] = normed.astype(BF)

        r2 = nf[...]
        for c in range(hidden // 512):
            cs = pl.ds(c * 512, 512)
            v = dot(nb[R, :], wu[:, cs]).astype(BF)
            v2 = v * v
            t = jnp.tanh(v * (BF(GELU_A) + BF(GELU_A * GELU_B) * v2))
            h = BF(0.5) + BF(0.5) * t
            active = v * h
            act[R, cs] = active
            gp[R, cs] = h + h * ((BF(1) - h) * (v * (BF(2 * GELU_A) + BF(6 * GELU_A * GELU_B) * v2)))
            r2 = r2 + dot(active, wd[cs, :])
        center = r2 - row_mean(r2)
        rstd = lax.rsqrt(row_mean(center * center) + EPSILON)
        unit = center * rstd
        tok[R, :] = (unit * g2[...] + b2[...]).astype(BF)
        up = cot[R, :].astype(F32)
        small[0:1, :] += jnp.sum(up * unit, axis=0, keepdims=True)
        small[1:2, :] += jnp.sum(up, axis=0, keepdims=True)
        e = up * g2[...]
        cot[R, :] = (rstd * (e - row_mean(e) - unit * row_mean(e * unit))).astype(BF)
        return 0

    lax.fori_loop(0, windows, feed, 0)
    out_copy = pltpu.make_async_copy(tok, out_h, out_sem.at[0])
    out_copy.start()

    def hooked(phase, body, count, first=0):
        def one(t, _):
            body(t, 0)
            for at in range(count):
                steps = SCHEDULE.get((phase, first + at))
                if steps:
                    pl.when(t == at)(functools.partial(run_steps, steps))
            return 0

        lax.fori_loop(0, count, one, 0)

    def run_steps(steps):
        for name, k in steps:
            if name == "sm":
                exchange_small(k)
            else:
                exchange(name, k)

    halves = hidden // 1024

    def down_tile(part, m, _):
        tile = m * halves + part
        d = dot(act[:, columns_of(tile * 512, 512)], cot[...], 0, 0).astype(BF).reshape(16, 32, 512)
        G["D%d" % part][m] = d
        return 0

    for part in range(2):
        hooked("down", functools.partial(down_tile, part), 2, 2 * part)

    def slope(w, _):
        R = rows_of(w, win)
        for c in range(hidden // 512):
            cs = pl.ds(c * 512, 512)
            d = dot(cot[R, :], wd[pl.ds(c * 512, 512), :], 1, 1)
            gp[R, cs] = (d * gp[R, cs].astype(F32)).astype(BF)
        return 0

    hooked("slope", slope, windows)

    def up_tile(part, m, _):
        tile = m * halves + part
        d = dot(nb[...], gp[:, columns_of(tile * 512, 512)], 0, 0).astype(BF).reshape(16, 32, 512)
        G["U%d" % part][m] = d
        return 0

    for part in range(2):
        hooked("up", functools.partial(up_tile, part), 2, 2 * part)

    def norm_back(w, _):
        R = rows_of(w, win)
        ng = cot[R, :].astype(F32) + dot(gp[R, :], wu[...], 1, 1)
        unit = u1[R, :].astype(F32)
        small[2:3, :] += jnp.sum(ng * unit, axis=0, keepdims=True)
        small[3:4, :] += jnp.sum(ng, axis=0, keepdims=True)
        e = ng * g1[...]
        rstd = jnp.sum(jnp.where(lanes((win, 128)) == w, rs1[...], 0.0), axis=1, keepdims=True)
        rg = (rstd * (e - row_mean(e) - unit * row_mean(e * unit))).astype(BF)
        cot[R, :] = rg
        u1[R, :] = dot(rg, wo[...], 1, 1).astype(BF)
        return 0

    hooked("nb", norm_back, windows)

    G["O"][...] = dot(mix[...], cot[...], 0, 0).astype(BF).reshape(2, 16, half // 16, 512)
    run_steps(SCHEDULE.get(("O", 0), ()))

    flip = (lax.broadcasted_iota(jnp.int32, (256, 128), 0) % 128 < HD) != (lanes((256, 128)) < HD)
    swap = jnp.where(flip, 1.0, 0.0).astype(BF)

    def attend_back(w, p):
        R = rows_of(w, win)
        pc = columns_of(p * 128, 128)
        Q, K, V = (joined[R, columns_of(width * i + p * 128, 128)] for i in range(3))
        D = u1[R, pc]
        prod = D.astype(F32) * mix[R, pc].astype(F32)
        ph = prod.astype(BF)
        pr = (prod - ph.astype(F32)).astype(BF)
        x = -dot(jnp.concatenate([ph, pr], axis=1), swap)
        hi = x.astype(BF)
        mid = (x - hi.astype(F32)).astype(BF)
        zero = jnp.zeros((win, 128), BF)
        ad = jnp.where(l64 == 8, hi, jnp.where(l64 == 9, mid, zero))
        av = jnp.where((l64 == 8) | (l64 == 9), jnp.ones((win, 128), BF), zero)
        aq, ak = augq[R, pc], augk[R, :]
        QT, DT = Q.T, D.T
        probs, grads = [[], []], [[], []]
        for h in range(2):
            mine = lo if h == 0 else ~lo
            qa, ka, va, da = (jnp.where(mine, i, j) for i, j in ((Q, aq), (K, ak), (V, av), (D, ad)))
            for qb in range(2):
                kl = half * (qb + 1)
                qs = slice(qb * half, kl)
                s = dot(qa[qs], ka[:kl], 1, 1)
                s = s + causal if qb == 0 else jnp.concatenate([s[:, :half], s[:, half:] + causal], axis=1)
                e = jnp.exp(s)
                grads[h].append((e * dot(da[qs], va[:kl], 1, 1)).astype(BF))
                probs[h].append(e.astype(BF))
        dq, dk, dv = [None, None], [], []
        for h in range(2):
            km = jnp.where(lo if h == 0 else ~lo, K, zero)
            hs = slice(h * HD, (h + 1) * HD)
            for qb in range(2):
                x = dot(grads[h][qb], km[: half * (qb + 1)])
                dq[qb] = x if h == 0 else dq[qb] + x
            for left, (first, second), to in ((QT, grads[h], dk), (DT, probs[h], dv)):
                early = dot(left[hs], jnp.concatenate([first, second[:, :half]], axis=0))
                to.append(jnp.concatenate([early, dot(left[hs, half:], second[:, half:])], axis=1))
        for i in range(2):
            joined[pl.ds(pl.multiple_of(w * win + i * half, half), half), pc] = dq[i].astype(BF)
        for i, v in enumerate((dk, dv)):
            joined[R, columns_of(width * (i + 1) + p * 128, 128)] = jnp.concatenate(v, axis=0).astype(BF).T

    def qkv_grad(*some):
        def one(m, _):
            total = None
            for w in range(windows):
                R = pl.ds(w * win, win)
                right = jnp.concatenate(
                    [joined[R, pl.ds(width * i + p * 128, 128)] for p in some for i in range(3)], axis=1
                )
                d = dot(pb[R, columns_of(m * half, half)], right, 0, 0)
                total = d if total is None else total + d
            total = total.astype(BF)
            if len(some) == 2:
                for j in range(2):
                    G["Q0"][j, pl.ds(8 * m, 8)] = total[:, 384 * j : 384 * (j + 1)].reshape(8, 32, 384)
            else:
                G["QA" if some[0] == 1 else "QB"][m] = total.reshape(16, 16, 384)
            return 0

        lax.fori_loop(0, 2, one, 0)

    def add_position(p):
        cols = [pl.ds(width * i + p * 128, 128) for i in range(3)]
        total = []
        for c in cols:
            v = joined[pl.ds(0, win), c].astype(F32)
            for w in range(1, windows):
                v = v + joined[pl.ds(w * win, win), c].astype(F32)
            total.append(v.astype(BF))
        part = dot(jnp.concatenate(total, axis=1), jnp.concatenate([wq[:, c] for c in cols], axis=1), 1, 1)
        nf[...] = nf[...] + part

    def steps_at(phase, at):
        run_steps(SCHEDULE.get((phase, at), ()))

    total = cot[pl.ds(0, win), :].astype(F32)
    for w in range(1, windows):
        total = total + cot[pl.ds(w * win, win), :].astype(F32)
    nf[...] = total
    order = (0, 2, 1, 3)
    for i, p in enumerate(order):
        hooked("back%d" % i, lambda t, _: attend_back(t, p), windows)
        if i == 3:
            add_position(p)
            G["P"][...] = nf[...].astype(BF).reshape(2, 16, half // 16, 512)
            steps_at("P", 0)
        if i > 0:
            qkv_grad(*((0, 2) if i == 1 else (p,)))
        steps_at("q%d" % i, 0)
        if i < 3:
            add_position(p)
            steps_at("add%d" % i, 0)

    def finish(w, _):
        R = rows_of(w, win)
        cot[R, :] = (cot[R, :].astype(F32) + dot(joined[R, :], wq[...], 1, 1)).astype(BF)
        return 0

    hooked("fin", finish, windows)
    ig_copy = pltpu.make_async_copy(cot, ig_h, out_sem.at[1])
    ig_copy.start()
    small_copy = pltpu.make_async_copy(small, small_h, out_sem.at[2])
    small_copy.start()
    run_steps(TAIL)
    if fused:
        for name in NAMES:
            results_out(name, False)
    if not fused:
        outs = [pltpu.make_async_copy(G[nm], F[nm], in_sem.at[i]) for i, nm in enumerate(NAMES)]
        for c in outs:
            c.start()
        for c in outs:
            c.wait()
    out_copy.wait()
    ig_copy.wait()
    small_copy.wait()


def scratch_of(fused, dims):
    win, width, hidden, windows = dims
    rows = win * windows
    V, dma = pltpu.VMEM, pltpu.SemaphoreType.DMA
    b = {k: V((rows, width), BF) for k in ("tok", "cot", "mix", "u1", "pb", "nb", "augq")}
    b.update({k: V((rows, hidden), BF) for k in ("act", "gp")})
    b.update(
        pos=V((win, width), BF),
        augk=V((rows, 128), BF),
        wq=V((width, 3 * width), BF),
        wo=V((width, width), BF),
        wu=V((width, hidden), BF),
        wd=V((hidden, width), BF),
        joined=V((rows, 3 * width), BF),
        rs1=V((win, 128), F32),
        nf=V((win, width), F32),
        small=V((8, width), F32),
        in_sem=dma((12,)),
        out_sem=dma((3,)),
    )
    b.update({"G" + k: V((2, PIECES) + CHUNKS[k], BF) for k in NAMES})
    if fused:
        for k in NAMES:
            lead = {"M": (16,), "A": (8,), "B": (4,), "Z": (3,)}
            if k in DIRECT:
                lead = {"M": (16,), "A": (3, 4), "Z": (3,), "X": (16,)}
            b.update({buf + k: V(n + CHUNKS[k], BF) for buf, n in lead.items()})
        b.update({k: V((8, width), F32) for k in ("s_mp", "s_x", "s_y")})
        b.update(
            s_z=V((4, 8, width), F32),
            wsem=dma((2, 6)),
            csend=dma((len(NAMES), 15)),
            crecv=dma((len(NAMES), 15)),
            ssend=dma((6,)),
            srecv=dma((6,)),
            lsem=dma((2 * len(NAMES),)),
        )
    return b


def layer(fused, tok, cot, pos, seg, wq, wo, wu, wd, g1, b1, g2, b2, hidden):
    rows, width = tok.shape
    win = pos.shape[0]
    windows = rows // win
    hbm = pl.BlockSpec(memory_space=pl.ANY)
    vmem = pl.BlockSpec(memory_space=pltpu.VMEM)
    shape = jax.ShapeDtypeStruct
    full = {k: (PIECES,) + v if fused and k not in DIRECT else (2, PIECES) + v for k, v in CHUNKS.items()}
    full["Q1"] = full["QA"]
    outs = [shape((rows, width), BF), shape((rows, width), BF), shape((8, width), F32)]
    outs += [shape(full[k], BF) for k in (RESULTS if fused else NAMES)]
    scratch = list(scratch_of(fused, (win, width, hidden, windows)).values())
    params = dict(vmem_limit_bytes=64 << 20)
    if fused:
        params.update(collective_id=0, has_side_effects=True)
    return pl.pallas_call(
        functools.partial(kernel, fused, (win, width, hidden, windows)),
        out_shape=outs,
        in_specs=[hbm] * 3 + [vmem] + [hbm] * 4 + [vmem] * 4,
        out_specs=[hbm] * len(outs),
        scratch_shapes=scratch,
        compiler_params=pltpu.CompilerParams(**params),
        name="layer",
    )(tok, cot, pos, seg, wq, wo, wu, wd, g1, b1, g2, b2)


def widen(got, wide):
    rows = got.shape[-2]

    def one(i, _):
        piece = got[i] if len(got.shape) == 3 else got[i // PIECES, lax.rem(i, PIECES)]
        wide[pl.ds(pl.multiple_of(i * rows, rows), rows), :] = piece.astype(F32)
        return 0

    lax.fori_loop(0, wide.shape[0] // rows, one, 0)


def finish_kernel(*refs):
    (out_h, ig_h, small), grads = refs[:3], dict(zip(RESULTS, refs[3 : 3 + len(RESULTS)]))
    refs = refs[3 + len(RESULTS) :]
    out_o, ig_o, pos_o, qkv_o, wo_o, up_o, down_o = refs[:7]
    norms = refs[7:11]
    refs = refs[11:]
    got = dict(zip(RESULTS, refs[: len(RESULTS)]))
    wide = dict(zip(RESULTS, refs[len(RESULTS) : 2 * len(RESULTS)]))
    held, in_sem, out_sem = refs[2 * len(RESULTS) :]
    last, loads, passed = [], [], []
    for i, (src, dst) in enumerate(((out_h, out_o), (ig_h, ig_o))):
        passed.append(pltpu.make_async_copy(src, held.at[i], in_sem.at[len(RESULTS) + i]))
        last.append(pltpu.make_async_copy(held.at[i], dst, out_sem.at[len(RESULTS) + i]))
    for c in passed:
        c.start()
    for i, k in enumerate(RESULTS):
        loads.append(pltpu.make_async_copy(grads[k], got[k], in_sem.at[i]))
        loads[-1].start()
    rows = down_o.shape[0] // 2
    places = {
        "D0": down_o.at[pl.ds(0, rows)],
        "D1": down_o.at[pl.ds(rows, rows)],
        "U0": up_o.at[:, pl.ds(0, 512)],
        "U1": up_o.at[:, pl.ds(512, 512)],
        "O": wo_o,
        "Q0": qkv_o.at[:, pl.ds(0, 384)],
        "Q1": qkv_o.at[:, pl.ds(384, 384)],
        "P": pos_o,
    }
    for i in range(2):
        passed[i].wait()
        last[i].start()
    for i, k in enumerate(RESULTS):
        loads[i].wait()
        widen(got[k], wide[k])
        last.append(pltpu.make_async_copy(wide[k], places[k], out_sem.at[i]))
        last[-1].start()
    for ref, row in zip(norms, (2, 3, 0, 1)):
        ref[...] = small[row]
    for c in last:
        c.wait()


def finish(out, ig, small, grads, win, width, hidden):
    hbm = pl.BlockSpec(memory_space=pl.ANY)
    vmem = pl.BlockSpec(memory_space=pltpu.VMEM)
    shape = jax.ShapeDtypeStruct
    outs = [shape(out.shape, BF), shape(ig.shape, BF), shape((win, width), F32)]
    outs += [shape((width, 3 * width // 2), F32), shape((width // 2, width), F32)]
    outs += [shape((width, hidden // 2), F32), shape((hidden // 2, width), F32)]
    outs += [shape((width,), F32)] * 4
    dma = pltpu.SemaphoreType.DMA
    scratch = [pltpu.VMEM(g.shape, BF) for g in grads]
    scratch += [pltpu.VMEM((g.size // g.shape[-1], g.shape[-1]), F32) for g in grads]
    scratch += [pltpu.VMEM((2,) + out.shape, BF), dma((len(RESULTS) + 2,)), dma((len(RESULTS) + 2,))]
    return pl.pallas_call(
        finish_kernel,
        out_shape=outs,
        in_specs=[hbm, hbm, vmem] + [hbm] * len(RESULTS),
        out_specs=[hbm] * 7 + [vmem] * 4,
        scratch_shapes=scratch,
        compiler_params=pltpu.CompilerParams(vmem_limit_bytes=64 << 20),
        name="finish",
    )(out, ig, small, *grads)


def local(shards, tokens, segment_ids, cotangent, pos_table, w_qkv, w_out, w_up, w_down, g1, b1, g2, b2):
    dp_size, mp_size = shards
    width = tokens.shape[1]
    win = pos_table.shape[0]
    hidden = w_up.shape[1] * mp_size
    fused = dp_size == PIECES
    gains = [v.reshape(1, width) for v in (g1, b1, g2, b2)]
    if fused:
        out, ig, small, *grads = layer(
            True, tokens, cotangent, pos_table, segment_ids, w_qkv, w_out, w_up, w_down, *gains, hidden
        )
        return tuple(finish(out, ig, small, grads, win, width, hidden))
    windows = tokens.shape[0] // win
    seg = jnp.roll(segment_ids, -lax.axis_index("mp") * windows, axis=0)
    wq = lax.all_gather(w_qkv, "mp", axis=1, tiled=True)
    wo = lax.all_gather(w_out, "mp", axis=0, tiled=True)
    wu = lax.all_gather(w_up, "mp", axis=1, tiled=True)
    wd = lax.all_gather(w_down, "mp", axis=0, tiled=True)
    out, ig, small, *grads = layer(False, tokens, cotangent, pos_table, seg, wq, wo, wu, wd, *gains, hidden)
    g = dict(zip(NAMES, (v.astype(F32) for v in grads)))
    g = {
        k: v if k in DIRECT else lax.psum(lax.psum_scatter(v, "mp", scatter_dimension=0, tiled=False), "dp")
        for k, v in g.items()
    }
    pos, QA, QB, small = lax.psum((g["P"], g["QA"], g["QB"], small), ("dp", "mp"))
    g["Q1"] = jnp.where(lax.axis_index("mp") == 0, QA, QB)
    scale = jnp.array([HD**-0.5, 1, 1], F32)[:, None, None]
    Q = [(g[k].reshape(width, 3, 2, HD) * scale).transpose(0, 2, 1, 3).reshape(width, 6 * HD) for k in ("Q0", "Q1")]
    return (
        out,
        ig,
        pos.reshape(win, width),
        jnp.concatenate(Q, axis=1),
        g["O"].reshape(-1, width),
        jnp.concatenate([g["U0"].reshape(width, -1), g["U1"].reshape(width, -1)], axis=1),
        jnp.concatenate([g["D0"].reshape(-1, width), g["D1"].reshape(-1, width)], axis=0),
        small[2],
        small[3],
        small[0],
        small[1],
    )


def solution(mesh):
    cut, copied = P(("dp", "mp"), None), P()
    columns, split_rows = P(None, "mp"), P("mp", None)
    weights = (columns, split_rows, columns, split_rows)
    return jax.shard_map(
        functools.partial(local, (mesh.shape["dp"], mesh.shape["mp"])),
        mesh=mesh,
        in_specs=(cut, P("dp", None), cut, copied) + weights + (copied,) * 4,
        out_specs=(cut, cut, copied) + weights + (copied,) * 4,
        check_vma=False,
    )
```

profile of v0, /device:TPU:1, one launch (start us, length us, event | category | flops | bytes accessed | tf_op | source)
XLA Modules:
  0.0 137.1 jit_solution(16114510966056315943)
XLA Ops:
  0.6 128.4 %layer.1 = (bf16[2048,512]{1,0:T(8,128)(2,1)}, bf16[2048,512]{1,0:T(8,128)(2,1)}, f32[8,512]{1,0:T(8,128)}, bf16[16,32,512]{2,1,0:T(8,128)(2,1)}, bf16[16,32,512...) custom-call(bf16[2048,512]{1,0:T(8,128)(2,1)} %refs_0_.1, ...), custom_call_target="tpu_custom_call" | custom-call | tf_op jit(solution)/shard_map/layer/pallas_call | solution.py:697
  129.1 7.8 %finish.1 = (bf16[2048,512]{1,0:T(8,128)(2,1)}, bf16[2048,512]{1,0:T(8,128)(2,1)}, f32[512,512]{1,0:T(8,128)}, f32[512,768]{1,0:T(8,128)}, f32[256,512]{1,0:T(8,...) custom-call(bf16[2048,512]{1,0:T(8,128)(2,1)} %get-tuple-element.22., ...), custom_call_target="tpu_custom_call" | custom-call | tf_op jit(solution)/shard_map/finish/pallas_call | solution.py:774
where the time goes:
time: 137 us
  Pallas kernels  136 us (99%)
    pallas_call x1, Pallas kernels, layer(): pl.pallas_call(functools.partial(kernel, fused, (win, width, hidden, wind...  128 us
    pallas_call x1, Pallas kernels, finish(): pl.pallas_call(finish_kernel, out_shape=outs, in_specs=[hbm, hbm, vmem] +...  7.84 us

commit v1 on v0

--- a/solution.py
+++ b/solution.py
@@ -31,6 +31,7 @@
 DIRECT = ("QA", "QB", "P")
 RESULTS = ("D0", "D1", "U0", "U1", "O", "Q0", "Q1", "P")
 PIECES = 16
+UNROLLED = ("nb", )
 
 SCHEDULE = {
     ("down", 1): (("D0", 0),),
@@ -459,7 +460,12 @@
                     pl.when(t == at)(functools.partial(run_steps, steps))
             return 0
 
-        lax.fori_loop(0, count, one, 0)
+        if phase not in UNROLLED:
+            lax.fori_loop(0, count, one, 0)
+            return
+        for t in range(count):
+            body(t, 0)
+            run_steps(SCHEDULE.get((phase, t), ()))
 
     def run_steps(steps):
         for name, k in steps:

time: 137 us -> 137 us (level)
  no operation moved by 1% of the time
where the time goes in v1:
time: 137 us
  Pallas kernels  136 us (99%)
    pallas_call x1, Pallas kernels, layer(): pl.pallas_call(functools.partial(kernel, fused, (win, width, hidden, wind...  128 us
    pallas_call x1, Pallas kernels, finish(): pl.pallas_call(finish_kernel, out_shape=outs, in_specs=[hbm, hbm, vmem] +...  7.84 us

profile of v1, /device:TPU:1, one launch (start us, length us, event | category | flops | bytes accessed | tf_op | source)
XLA Modules:
  0.0 136.9 jit_solution(7785114144804883903)
XLA Ops:
  0.6 128.2 %layer.1 = (bf16[2048,512]{1,0:T(8,128)(2,1)}, bf16[2048,512]{1,0:T(8,128)(2,1)}, f32[8,512]{1,0:T(8,128)}, bf16[16,32,512]{2,1,0:T(8,128)(2,1)}, bf16[16,32,512...) custom-call(bf16[2048,512]{1,0:T(8,128)(2,1)} %refs_0_.1, ...), custom_call_target="tpu_custom_call" | custom-call | tf_op jit(solution)/shard_map/layer/pallas_call | solution.py:703
  128.9 7.8 %finish.1 = (bf16[2048,512]{1,0:T(8,128)(2,1)}, bf16[2048,512]{1,0:T(8,128)(2,1)}, f32[512,512]{1,0:T(8,128)}, f32[512,768]{1,0:T(8,128)}, f32[256,512]{1,0:T(8,...) custom-call(bf16[2048,512]{1,0:T(8,128)(2,1)} %get-tuple-element.22., ...), custom_call_target="tpu_custom_call" | custom-call | tf_op jit(solution)/shard_map/finish/pallas_call | solution.py:780

commit v2 on v1

--- a/solution.py
+++ b/solution.py
@@ -35,47 +35,45 @@
 
 SCHEDULE = {
     ("down", 1): (("D0", 0),),
-    ("down", 3): (("D1", 0),),
-    ("slope", 0): (("D0", 1),),
-    ("slope", 1): (("D1", 1),),
-    ("up", 1): (("D0", 2), ("U0", 0),),
+    ("down", 3): (("D0", 1), ("D1", 0),),
+    ("slope", 2): (("D1", 1),),
+    ("up", 0): (("D0", 2),),
+    ("up", 1): (("U0", 0),),
     ("up", 3): (("D1", 2), ("U0", 1), ("U1", 0),),
     ("nb", 0): (("D0", 3),),
     ("nb", 1): (("U1", 1),),
     ("nb", 2): (("D1", 3),),
     ("nb", 3): (("D0", 4), ("U0", 2),),
     ("O", 0): (("O", 0), ("sm", 0),),
-    ("back0", 1): (("D1", 4), ("U1", 2), ("O", 1), ("sm", 1),),
+    ("back0", 0): (("U1", 2),),
+    ("back0", 1): (("D1", 4), ("O", 1), ("sm", 1),),
     ("back0", 2): (("U0", 3),),
     ("back0", 3): (("D0", 5),),
-    ("back1", 0): (("sm", 2),),
-    ("back1", 1): (("D1", 5), ("U1", 3),),
-    ("back1", 2): (("O", 2),),
-    ("back1", 3): (("D0", 6), ("U0", 4), ("sm", 3),),
-    ("q1", 0): (("D1", 6), ("U1", 4), ("Q0", 0),),
-    ("add1", 0): (("O", 3),),
-    ("back2", 0): (("sm", 4),),
-    ("back2", 1): (("U0", 5), ("Q0", 1),),
-    ("back2", 2): (("D0", 7),),
-    ("back2", 3): (("U1", 5),),
-    ("q2", 0): (("D1", 7), ("O", 4), ("QA", 0),),
-    ("add2", 0): (("U0", 6),),
-    ("back3", 1): (("Q0", 2), ("QA", 1),),
-    ("back3", 2): (("U1", 6), ("O", 5),),
-    ("P", 0): (("P", 0),),
-    ("q3", 0): (("U0", 7), ("Q0", 3), ("QB", 0),),
-    ("fin", 0): (("QA", 2), ("P", 1),),
-    ("fin", 1): (("QB", 1),),
+    ("back1", 0): (("U1", 3), ("sm", 2),),
+    ("back1", 1): (("D1", 5), ("O", 2),),
+    ("back1", 2): (("U0", 4),),
+    ("back1", 3): (("D0", 6), ("sm", 3),),
+    ("q1", 0): (("D1", 6), ("U1", 4), ("O", 3), ("Q0", 0),),
+    ("back2", 0): (("U0", 5), ("sm", 4),),
+    ("back2", 1): (("Q0", 1),),
+    ("back2", 2): (("D0", 7), ("U1", 5),),
+    ("back2", 3): (("O", 4),),
+    ("q2", 0): (("D1", 7), ("U0", 6), ("QA", 0),),
+    ("back3", 1): (("O", 5), ("Q0", 2), ("QA", 1),),
+    ("back3", 2): (("U1", 6),),
+    ("P", 0): (("U0", 7), ("P", 0),),
+    ("q3", 0): (("O", 6), ("Q0", 3), ("QB", 0),),
+    ("fin", 0): (("P", 1),),
+    ("fin", 1): (("QA", 2), ("QB", 1),),
     ("fin", 3): (("U1", 7), ("Q0", 4),),
 }
 TAIL = (
-    ("O", 6),
     ("QA", 3),
+    ("O", 7),
     ("P", 2),
     ("Q0", 5),
+    ("QA", 4),
     ("QB", 2),
-    ("QA", 4),
-    ("O", 7),
     ("P", 3),
     ("QB", 3),
     ("Q0", 6),

time: 137 us -> 135 us (0.985)
  Pallas kernels: 136 us -> 134 us
    pallas_call x1, Pallas kernels: 128 us -> 126 us  [layer(): pl.pallas_call(functools.partial(kernel, fused, (win, width, hidden, wind...]
where the time goes in v2:
time: 135 us
  Pallas kernels  134 us (99%)
    pallas_call x1, Pallas kernels, layer(): pl.pallas_call(functools.partial(kernel, fused, (win, width, hidden, wind...  126 us
    pallas_call x1, Pallas kernels, finish(): pl.pallas_call(finish_kernel, out_shape=outs, in_specs=[hbm, hbm, vmem] +...  7.84 us

profile of v2, /device:TPU:1, one launch (start us, length us, event | category | flops | bytes accessed | tf_op | source)
XLA Modules:
  0.0 134.9 jit_solution(9158128573392602753)
XLA Ops:
  0.6 126.2 %layer.1 = (bf16[2048,512]{1,0:T(8,128)(2,1)}, bf16[2048,512]{1,0:T(8,128)(2,1)}, f32[8,512]{1,0:T(8,128)}, bf16[16,32,512]{2,1,0:T(8,128)(2,1)}, bf16[16,32,512...) custom-call(bf16[2048,512]{1,0:T(8,128)(2,1)} %refs_0_.1, ...), custom_call_target="tpu_custom_call" | custom-call | tf_op jit(solution)/shard_map/layer/pallas_call | solution.py:701
  126.9 7.8 %finish.1 = (bf16[2048,512]{1,0:T(8,128)(2,1)}, bf16[2048,512]{1,0:T(8,128)(2,1)}, f32[512,512]{1,0:T(8,128)}, f32[512,768]{1,0:T(8,128)}, f32[256,512]{1,0:T(8,...) custom-call(bf16[2048,512]{1,0:T(8,128)(2,1)} %get-tuple-element.22., ...), custom_call_target="tpu_custom_call" | custom-call | tf_op jit(solution)/shard_map/finish/pallas_call | solution.py:778

commit v3 on v2

--- a/solution.py
+++ b/solution.py
@@ -35,52 +35,51 @@
 
 SCHEDULE = {
     ("down", 1): (("D0", 0),),
-    ("down", 3): (("D0", 1), ("D1", 0),),
-    ("slope", 2): (("D1", 1),),
+    ("down", 3): (("D1", 0), ("D0", 1),),
+    ("slope", 1): (("D1", 1),),
     ("up", 0): (("D0", 2),),
     ("up", 1): (("U0", 0),),
-    ("up", 3): (("D1", 2), ("U0", 1), ("U1", 0),),
+    ("up", 2): (("D1", 2),),
+    ("up", 3): (("U1", 0), ("U0", 1),),
     ("nb", 0): (("D0", 3),),
-    ("nb", 1): (("U1", 1),),
-    ("nb", 2): (("D1", 3),),
-    ("nb", 3): (("D0", 4), ("U0", 2),),
-    ("O", 0): (("O", 0), ("sm", 0),),
-    ("back0", 0): (("U1", 2),),
-    ("back0", 1): (("D1", 4), ("O", 1), ("sm", 1),),
-    ("back0", 2): (("U0", 3),),
-    ("back0", 3): (("D0", 5),),
-    ("back1", 0): (("U1", 3), ("sm", 2),),
-    ("back1", 1): (("D1", 5), ("O", 2),),
-    ("back1", 2): (("U0", 4),),
-    ("back1", 3): (("D0", 6), ("sm", 3),),
-    ("q1", 0): (("D1", 6), ("U1", 4), ("O", 3), ("Q0", 0),),
-    ("back2", 0): (("U0", 5), ("sm", 4),),
-    ("back2", 1): (("Q0", 1),),
-    ("back2", 2): (("D0", 7), ("U1", 5),),
-    ("back2", 3): (("O", 4),),
-    ("q2", 0): (("D1", 7), ("U0", 6), ("QA", 0),),
-    ("back3", 1): (("O", 5), ("Q0", 2), ("QA", 1),),
-    ("back3", 2): (("U1", 6),),
-    ("P", 0): (("U0", 7), ("P", 0),),
-    ("q3", 0): (("O", 6), ("Q0", 3), ("QB", 0),),
-    ("fin", 0): (("P", 1),),
-    ("fin", 1): (("QA", 2), ("QB", 1),),
-    ("fin", 3): (("U1", 7), ("Q0", 4),),
+    ("nb", 1): (("U1", 1), ("D1", 3),),
+    ("nb", 3): (("U0", 2), ("D0", 4),),
+    ("O", 0): (("sm", 0), ("O", 0),),
+    ("back0", 0): (("U1", 2), ("D1", 4),),
+    ("back0", 1): (("sm", 1), ("O", 1),),
+    ("back0", 2): (("U0", 3), ("D0", 5),),
+    ("back1", 0): (("sm", 2), ("U1", 3), ("D1", 5),),
+    ("back1", 1): (("O", 2),),
+    ("back1", 2): (("U0", 4), ("D0", 6),),
+    ("back1", 3): (("sm", 3),),
+    ("q1", 0): (("Q0", 0), ("O", 3), ("U1", 4), ("D1", 6),),
+    ("back2", 0): (("sm", 4), ("U0", 5),),
+    ("back2", 1): (("Q0", 1), ("O", 4), ("D0", 7),),
+    ("back2", 3): (("U1", 5),),
+    ("q2", 0): (("QA", 0), ("O", 5), ("U0", 6), ("D1", 7),),
+    ("back3", 1): (("QA", 1), ("Q0", 2),),
+    ("back3", 2): (("O", 6), ("U1", 6),),
+    ("P", 0): (("P", 0),),
+    ("q3", 0): (("QB", 0), ("U0", 7),),
+    ("fin", 0): (("P", 1), ("QA", 2),),
+    ("fin", 1): (("QB", 1), ("Q0", 3),),
+    ("fin", 2): (("O", 7),),
+    ("fin", 3): (("QA", 3),),
 }
 TAIL = (
-    ("QA", 3),
-    ("O", 7),
+    ("U1", 7),
+    ("Q0", 4),
+    ("QA", 4),
     ("P", 2),
+    ("QB", 2),
     ("Q0", 5),
-    ("QA", 4),
-    ("QB", 2),
     ("P", 3),
+    ("QA", 5),
     ("QB", 3),
+    ("QA", 6),
     ("Q0", 6),
     ("P", 4),
-    ("QA", 5),
     ("QB", 4),
-    ("QA", 6),
     ("Q0", 7),
     ("P", 5),
     ("P", 6),

time: 135 us -> 135 us (level)
  no operation moved by 1% of the time
where the time goes in v3:
time: 135 us; the launch traced here: 134 us
  Pallas kernels  134 us (99%)
    pallas_call x1, Pallas kernels, layer(): pl.pallas_call(functools.partial(kernel, fused, (win, width, hidden, wind...  126 us
    pallas_call x1, Pallas kernels, finish(): pl.pallas_call(finish_kernel, out_shape=outs, in_specs=[hbm, hbm, vmem] +...  7.84 us

profile of v3, /device:TPU:1, one launch (start us, length us, event | category | flops | bytes accessed | tf_op | source)
XLA Modules:
  0.0 134.5 jit_solution(7062388782762467689)
XLA Ops:
  0.6 125.8 %layer.1 = (bf16[2048,512]{1,0:T(8,128)(2,1)}, bf16[2048,512]{1,0:T(8,128)(2,1)}, f32[8,512]{1,0:T(8,128)}, bf16[16,32,512]{2,1,0:T(8,128)(2,1)}, bf16[16,32,512...) custom-call(bf16[2048,512]{1,0:T(8,128)(2,1)} %refs_0_.1, ...), custom_call_target="tpu_custom_call" | custom-call | tf_op jit(solution)/shard_map/layer/pallas_call | solution.py:700
  126.5 7.8 %finish.1 = (bf16[2048,512]{1,0:T(8,128)(2,1)}, bf16[2048,512]{1,0:T(8,128)(2,1)}, f32[512,512]{1,0:T(8,128)}, f32[512,768]{1,0:T(8,128)}, f32[256,512]{1,0:T(8,...) custom-call(bf16[2048,512]{1,0:T(8,128)(2,1)} %get-tuple-element.22., ...), custom_call_target="tpu_custom_call" | custom-call | tf_op jit(solution)/shard_map/finish/pallas_call | solution.py:777
